TPU v7x, 256 devices: a whole 4x4x8 slice. The times are simulated.
256 devices in a mesh: aux: 8 (over z_hi, y), pair: 32 (over x, z_lo, core).
Axes of the slice: x: 4, y: 4, z: 8 (z_hi: 2, z_lo: 4; z = z_hi * 4 + z_lo), core: 2. Of those that a mesh axis runs over, the one named last changes fastest.
Arguments:
- density: bfloat16 [28800, 28800], P('aux', 'pair'), may hold values from -0.03125 to 0.03125
- cholesky: bfloat16 [512, 28800], P('pair', 'aux'), may hold values from -6 to 6
- virtual_orbitals: bfloat16 [3000, 1800], P('aux'), may hold values from -0.125 to 0.125
- occupied_orbitals: bfloat16 [128, 16], replicated, may hold values from -1.5 to 1.5
Outputs:
- back_transformed: bfloat16 [512, 128, 3000], P('pair', None, 'aux')
- lagrangian: float32 [16, 16], P(None, 'aux')
All inputs are finite; a program needn't handle non-finite values.
Results may differ from a plain program's by a relative error of at most 0.0057.
Values may be sent and summed in bfloat16 or wider, within the bound.
A program may use at most 64 MiB of HBM per device.

v0:
```python
import jax
import jax.numpy as jnp
from jax import lax
from jax.sharding import PartitionSpec as P

NCHOL = 512


def on_device(density, cholesky, virtual_orbitals, occupied_orbitals):
    partial_value = jnp.dot(
        lax.all_gather(cholesky, "pair", axis=0, tiled=True),
        density,
        preferred_element_type=jnp.float32,
    )
    summed = lax.psum(partial_value, "aux")
    vectors = lax.all_to_all(
        summed.astype(jnp.bfloat16), "pair", split_axis=0, concat_axis=1, tiled=True
    )
    occupied = occupied_orbitals.shape[1]
    virtual = virtual_orbitals.shape[1]
    blocked = vectors.reshape(vectors.shape[0], occupied, virtual)
    half_done = jnp.einsum(
        "kia,na->kin", blocked, virtual_orbitals, preferred_element_type=jnp.float32
    ).astype(jnp.bfloat16)
    back_transformed = jnp.einsum(
        "mi,kin->kmn", occupied_orbitals, half_done, preferred_element_type=jnp.float32
    ).astype(jnp.bfloat16)
    local_vectors = cholesky.reshape(cholesky.shape[0], cholesky.shape[1] // virtual, virtual)
    lag_terms = (
        jnp.einsum("kib,kjb->ij", blocked, local_vectors, preferred_element_type=jnp.float32)
        / NCHOL
    )
    lagrangian = lax.psum(lag_terms, "pair")
    return (back_transformed, lagrangian)


def solution(mesh):
    return jax.shard_map(
        on_device,
        mesh=mesh,
        in_specs=(P("aux", "pair"), P("pair", "aux"), P("aux", None), P()),
        out_specs=(P("pair", None, "aux"), P(None, "aux")),
        check_vma=False,
    )
```

profile of v0, /device:TPU:1, one launch (start us, length us, event | category | flops | bytes accessed | tf_op | source)
XLA Modules:
  0.0 317.0 jit_solution(4154199917977561640)
XLA Ops:
  7.2 0.0 copy-start
  7.2 0.0 all-gather.2.cloned.1.call-start
  7.2 0.7 all-gather.2.cloned.1.call-update
  7.9 68.7 %all-gather.2.cloned.1.call-done = bf16[512,3600]{1,0:T(8,128)(2,1)} async-done(((bf16[16,3600]{1,0:T(8,128)(2,1)}), bf16[512,3600]{1,0:T(8,128)(2,1)}) %all-gather.2.cloned.1.call-update) | async-done | bytes 3686416 | tf_op jit(solution)/shard_map/all_gather | solution.py:11
  76.6 9.1 %fusion.10 = f32[512,900]{0,1:T(8,128)} fusion(bf16[512,3600]{1,0:T(8,128)(2,1)} %all-gather.2.cloned.1.call-done, bf16[3600,900]{0,1:T(8,128)(2,1)} %param.4), kind=kOutput, calls=%fused_computation.8 | convolution fusion | flops 3317760000 | bytes 12009600 | tf_op jit(solution)/shard_map/dot_general | solution.py:10
  85.7 99.6 %all-reduce.1 = bf16[512,900]{0,1:T(8,128)(2,1)S(1)} all-reduce(f32[512,900]{0,1:T(8,128)} %fusion.10), channel_id=1, replica_groups=mesh['aux'=8,'pair'=32] {'aux'}, use_global_device_ids=true, to_apply=%region_0.0 | all-reduce | flops 460800 | bytes 2764800 | tf_op jit(solution)/shard_map/psum | solution.py:15
  185.3 0.0 copy-start.2
  185.4 1.3 copy.8
  186.7 21.0 %all-to-all-start = ((bf16[32,16,900]{2,1,0:T(8,128)(2,1)}), bf16[32,16,900]{2,1,0:T(8,128)(2,1)S(1)}, u32[]{:S(2)}, u32[]{:S(2)}) async-start(bf16[32,16,900]{2,1,0:T(8,128)(2,1)} %bitcast), calls=%async_computation | async-start | bytes 2097152 | tf_op jit(solution)/shard_map/all_to_all | solution.py:16
  207.7 0.0 copy-done.2
  207.7 0.8 reshape.15
  208.5 27.1 %all-to-all-done = bf16[32,16,900]{2,1,0:T(8,128)(2,1)S(1)} async-done(((bf16[32,16,900]{2,1,0:T(8,128)(2,1)}), bf16[32,16,900]{2,1,0:T(8,128)(2,1)S(1)}, u32[]{:S(2)}, u32[]{:S(2)}) %all-to-all-start) | async-done | bytes 921632 | tf_op jit(solution)/shard_map/all_to_all | solution.py:16
  235.5 0.6 copy.9
  236.1 0.0 copy-start.3
  236.1 0.7 reshape.14
  236.9 0.0 copy-start.1
  236.9 1.5 fusion.8
  238.3 0.0 copy-done.1
  238.3 67.6 %psum.15 = f32[16,2]{0,1:T(2,128)} all-reduce(f32[16,2]{0,1:T(2,128)S(1)} %fusion.8), channel_id=1, replica_groups=mesh['aux'=8,'pair'=32] {'pair'}, use_global_device_ids=true, to_apply=%region_1.0 | all-reduce | flops 32 | bytes 256 | tf_op jit(solution)/shard_map/psum | solution.py:33
  305.9 0.0 copy-done
  305.9 0.0 copy-done.3
  305.9 2.9 fusion
  308.8 1.3 copy.10
Async XLA Ops:
  7.2 298.8 %copy-start = (bf16[375,1800]{0,1:T(8,128)(2,1)S(1)}, bf16[375,1800]{0,1:T(8,128)(2,1)}, u32[]{:S(2)}) copy-start(bf16[375,1800]{0,1:T(8,128)(2,1)} %param.6) | copy-start | bytes 4050004
  7.2 69.4 %all-gather.2.cloned.1.call-start = ((), (), s32[]{:S(2)}) async-start(), calls=%async_computation.1 | async-start | bytes 3919872 | tf_op jit(solution)/shard_map/all_gather | solution.py:11
  185.3 22.3 %copy-start.2 = (bf16[16,3600]{1,0:T(8,128)(2,1)S(1)}, bf16[16,3600]{1,0:T(8,128)(2,1)}, u32[]{:S(2)}) copy-start(bf16[16,3600]{1,0:T(8,128)(2,1)} %param.5) | copy-start | bytes 345604
  186.7 48.9 %all-to-all-start = ((bf16[32,16,900]{2,1,0:T(8,128)(2,1)}), bf16[32,16,900]{2,1,0:T(8,128)(2,1)S(1)}, u32[]{:S(2)}, u32[]{:S(2)}) async-start(bf16[32,16,900]{2,1,0:T(8,128)(2,1)} %bitcast), calls=%async_computation | async-start | bytes 2097152 | tf_op jit(solution)/shard_map/all_to_all | solution.py:16
  236.1 69.8 %copy-start.3 = (bf16[128,16]{0,1:T(8,128)(2,1)S(1)}, bf16[128,16]{0,1:T(8,128)(2,1)}, u32[]{:S(2)}) copy-start(bf16[128,16]{0,1:T(8,128)(2,1)} %param.7) | copy-start | bytes 12292
  236.9 1.5 copy-start.1
Sparse Core Ops, SparseCore 0:
  9.9 66.7 all-gather.1
where the time goes:
time: 317 us
  blocking collectives  167 us (53%)
  waiting for transfers between devices  96.5 us (30%)
  starting transfers between devices  21 us (7%)
  between operations  14.1 us (4%)
  matrix products  13.5 us (4%)
  local copies, waits for them, and re-layouts  4.78 us (2%)
    psum x1, blocking collectives, on_device(): summed = lax.psum(partial_value, 'aux')  99.6 us
    all_gather x1, waiting for transfers between devices, on_device(): lax.all_gather(cholesky, 'pair', axis=0, tiled=True)  68.7 us
    psum x1, blocking collectives, on_device(): lagrangian = lax.psum(lag_terms, 'pair')  67.6 us
    all_to_all x1, waiting for transfers between devices, on_device(): lax.all_to_all(summed.astype(jnp.bfloat16), 'pair', split_axis=0, concat_...  27.1 us
    all_to_all x1, starting transfers between devices, on_device(): lax.all_to_all(summed.astype(jnp.bfloat16), 'pair', split_axis=0, concat_...  21 us
    dot_general x1, matrix products, on_device(): jnp.dot(lax.all_gather(cholesky, 'pair', axis=0, tiled=True), density, pr...  9.11 us
  transfers between devices with their start and end apart: 2, of which 2 were waited for; matrix products, arithmetic and copies ran while one was open for 0% of the time, Pallas kernels for 0%

commit v1 on v0

v1 whole, which is shorter than its diff:
```python
import jax
import jax.numpy as jnp
from jax import lax
from jax.experimental import pallas as pl
from jax.experimental.pallas import tpu as pltpu
from jax.sharding import PartitionSpec as P

MESH = pl.DeviceIdType.MESH
F32 = jnp.float32
BF16 = jnp.bfloat16
NT = (((1,), (1,)), ((), ()))

NX, NY, NZ, NC = 4, 4, 4, 2
ROWS = 16
CUTS = (0, 224, 448, 672, 900)
WIDE = 256
COLUMN = (0, 1, 3, 2)
BACK = (0, 2, 1, 3)
NCHOL = 512


def kernel(
    dt_hbm, chol_hbm, virt_hbm, occ_hbm, out_ref, lag_ref,
    gath, dt, virt, occ, virtp, lc, weights, part, fromy, summed, owned, gamma, half, lagrow, lagmine, lagall,
    local_sem, bulk_sem, block_sem, y_sem, own_sem, g_sem, lag_sem,
    send_block, send_y, send_own, send_g, send_lag,
):
    aux, pair = lax.axis_index("aux"), lax.axis_index("pair")
    zh, y = aux // NY, aux % NY
    x, zl, c = pair // (NZ * NC), (pair // NC) % NZ, pair % NC
    me = c * NZ + zl

    def device(zh_, y_, x_, zl_, c_):
        return (zh_ * NY + y_, (x_ * NZ + zl_) * NC + c_)

    barrier = pltpu.get_barrier_semaphore()
    own_place = zh * 32 + pair

    def greet(t, carry):
        @pl.when(t != own_place)
        def _():
            pl.semaphore_signal(barrier, inc=1, device_id=((t // 32) * NY + y, t % 32), device_id_type=MESH)

        return carry

    lax.fori_loop(0, 64, greet, 0)
    for dy in range(1, NY):
        pl.semaphore_signal(barrier, inc=1, device_id=(zh * NY + (y + dy) % NY, pair), device_id_type=MESH)

    own = pltpu.make_async_copy(chol_hbm, gath.at[0, me], local_sem.at[0])
    own.start()
    load_virt = pltpu.make_async_copy(virt_hbm, virt, local_sem.at[1])
    load_virt.start()
    load_occ = pltpu.make_async_copy(occ_hbm, occ, local_sem.at[2])
    load_occ.start()
    load_dt = pltpu.make_async_copy(dt_hbm, dt, bulk_sem)
    load_dt.start()
    own.wait()
    pl.semaphore_wait(barrier, 66)

    def block(src_k, dst_k, j, target):
        return pltpu.make_async_remote_copy(
            src_ref=gath.at[src_k, j], dst_ref=gath.at[dst_k, j], send_sem=send_block,
            recv_sem=block_sem.at[dst_k, j], device_id=target, device_id_type=MESH,
        )

    right = device(zh, y, (x + 1) % NX, zl, c)
    left = device(zh, y, (x + NX - 1) % NX, zl, c)
    sibling = device(zh, y, x, zl, 1 - c)
    up = device(zh, y, x, (zl + 1) % NZ, c)
    down = device(zh, y, x, (zl + NZ - 1) % NZ, c)

    def arrived(k, j):
        pltpu.make_async_copy(gath.at[k, j], gath.at[k, j], block_sem.at[k, j]).wait()

    pick = lambda a, b, c_, d: jnp.where(zl == 0, a, jnp.where(zl == 1, b, jnp.where(zl == 2, c_, d)))
    order = (zl, pick(1, 2, 3, 2), pick(2, 0, 1, 1), pick(3, 3, 0, 0))

    def along_x(j):
        block(0, 2, j, right).start()
        block(0, 1, j, left).start()
        block(0, 0, j, sibling).start()

    def own_column(q):
        j = c * NZ + order[q]
        if q == 0:
            @pl.when(zl < NZ - 1)
            def _():
                block(0, 0, j, up).start()

            @pl.when(zl > 0)
            def _():
                block(0, 0, j, down).start()
        else:
            arrived(0, j)

            @pl.when((order[q] < zl) & (zl < NZ - 1))
            def _():
                block(0, 0, j, up).start()

            @pl.when((order[q] > zl) & (zl > 0))
            def _():
                block(0, 0, j, down).start()

        along_x(j)

    def beside(q):
        j = c * NZ + order[q]
        arrived(1, j)
        if q % 2 == 1:
            block(1, 3, j, left).start()
        block(1, 1, j, sibling).start()
        arrived(2, j)
        if q % 2 == 0:
            block(2, 3, j, right).start()
        block(2, 2, j, sibling).start()

    def opposite(q):
        j = c * NZ + order[q]
        arrived(3, j)
        block(3, 3, j, sibling).start()

    def from_sibling(k):
        for z in range(NZ):
            arrived(k, (1 - c) * NZ + z)

    def product(k, n):
        rows = gath[pl.ds(k, n)].reshape(n * 128, 3600)
        for cut in range(NY):
            width = CUTS[cut + 1] - CUTS[cut]
            value = lax.dot_general(rows, dt[pl.ds(CUTS[cut], width), :], NT, preferred_element_type=F32).astype(BF16)
            for m in range(n):
                part[k + m, cut, :, 0:width] = value[m * 128 : (m + 1) * 128]
        for m in range(n):
            for dy in range(1, NY):
                over_y(k + m, dy).start()

    def over_y(k, dy):
        to = (y + dy) % NY
        return pltpu.make_async_remote_copy(
            src_ref=part.at[k, to], dst_ref=fromy.at[k, dy - 1], send_sem=send_y, recv_sem=y_sem.at[k, dy - 1],
            device_id=(zh * NY + to, pair), device_id_type=MESH,
        )

    def to_owner(k, t):
        tz, j = t // 8, t % 8
        return pltpu.make_async_remote_copy(
            src_ref=summed.at[k, j], dst_ref=owned.at[BACK[k], zh, me], send_sem=send_own, recv_sem=own_sem.at[BACK[k]],
            device_id=device(tz, y, (x + COLUMN[k]) % NX, j % NZ, j // NZ), device_id_type=MESH,
        )

    def sum_y(k):
        total = part[k, y].astype(F32)
        for dy in range(1, NY):
            over_y(k, dy).wait_recv()
            total = total + fromy[k, dy - 1].astype(F32)
        summed[k] = total.astype(BF16).reshape(8, ROWS, WIDE)

        def send(t, carry):
            t = (t + zh * 8 + me) % 16
            if k == 0:
                @pl.when(t != zh * 8 + me)
                def _():
                    to_owner(k, t).start()

                @pl.when(t == zh * 8 + me)
                def _():
                    pltpu.make_async_copy(summed.at[k, me], owned.at[0, zh, me], own_sem.at[0]).start()
            else:
                to_owner(k, t).start()
            return carry

        lax.fori_loop(0, 16, send, 0)

    def gather_y(k, dy):
        return pltpu.make_async_remote_copy(
            src_ref=gamma.at[k, y], dst_ref=gamma.at[k, y], send_sem=send_g, recv_sem=g_sem.at[k, dy - 1],
            device_id=(zh * NY + (y + dy) % NY, pair), device_id_type=MESH,
        )

    def complete(k):
        pltpu.make_async_copy(owned.at[k], owned.at[k], own_sem.at[k]).wait()
        gamma[k, y] = (owned[k, 0].astype(F32) + owned[k, 1].astype(F32)).astype(BF16)
        for dy in range(1, NY):
            gather_y(k, dy).start()

    def transform(k):
        for dy in range(1, NY):
            gather_y(k, dy).wait_recv()
        total = jnp.zeros((64, 375), F32)
        for h in range(2):
            for cut in range(NY):
                total = total + jnp.dot(
                    gamma[k, cut, pl.ds(4 * h, 4)].reshape(64, WIDE), virtp[4 * h + cut], preferred_element_type=F32
                )
        half[k] = total
        for z in range(NZ):
            i = ((x + COLUMN[k]) % NX) * NZ + z
            for j in range(2):
                terms = jnp.zeros((ROWS, WIDE), F32)
                for h in range(2):
                    for cut in range(NY):
                        terms = terms + gamma[k, cut, 4 * h + z].astype(F32) * lc[j, 4 * h + cut]
                terms = terms[:, :128] + terms[:, 128:]
                lagrow[j, pl.ds(i, 1), :] = jnp.sum(terms, axis=0, keepdims=True)

    own_column(0)

    part[:, :, :, 128:256] = jnp.zeros((4, NY, 128, 128), BF16)
    virtp[...] = jnp.zeros(virtp.shape, BF16)
    lc[...] = jnp.zeros(lc.shape, F32)
    lagmine[...] = jnp.zeros(lagmine.shape, F32)
    load_virt.wait()
    load_occ.wait()
    for h in range(2):
        for cut in range(NY):
            width = CUTS[cut + 1] - CUTS[cut]
            start = h * 900 + CUTS[cut]
            first = start // 8 * 8
            value = virt[first : start + width, :].astype(F32)
            virtp[4 * h + cut, 0:width, :] = value[start - first :].astype(BF16)
    mine = gath[0, me].astype(F32)
    for j in range(2):
        for h in range(2):
            for cut in range(NY):
                width = CUTS[cut + 1] - CUTS[cut]
                start = j * 1800 + h * 900 + CUTS[cut]
                lc[j, 4 * h + cut, :, 0:width] = mine[:, start : start + width]
    for k in range(4):
        for z in range(NZ):
            i = ((x + COLUMN[k]) % NX) * NZ + z
            row = occ[pl.ds(i, 1), :]
            weights[pl.ds(k * 64 + z * 16, 16), :] = jnp.broadcast_to(row, (16, 128)).astype(BF16)

    own_column(1)
    beside(0)
    own_column(2)
    beside(1)
    own_column(3)
    beside(2)
    from_sibling(0)
    load_dt.wait()
    product(0, 1)
    beside(3)
    from_sibling(1)
    from_sibling(2)
    product(1, 2)
    sum_y(0)
    for q in range(4):
        opposite(q)
    sum_y(1)
    sum_y(2)
    complete(0)
    from_sibling(3)
    product(3, 1)
    complete(1)
    complete(2)
    transform(0)
    sum_y(3)
    transform(1)
    transform(2)
    complete(3)
    transform(3)

    lagmine[0:2, 0:16] = jnp.sum(lagrow[...], axis=-1) * (1.0 / NCHOL)

    def share(t, carry):
        to = (pair + t) % 32
        pltpu.make_async_remote_copy(
            src_ref=lagmine, dst_ref=lagall.at[pair], send_sem=send_lag, recv_sem=lag_sem,
            device_id=(aux, to), device_id_type=MESH,
        ).start()
        return carry

    pltpu.make_async_copy(lagmine, lagall.at[pair], lag_sem).start()
    lax.fori_loop(1, 32, share, 0)

    turned = half[...].reshape(256, 375).astype(BF16).astype(F32).T
    row = lax.broadcasted_iota(jnp.int32, (ROWS, 256), 0)
    lane = lax.broadcasted_iota(jnp.int32, (ROWS, 256), 1)
    keep = (lane % ROWS) == row
    for start in range(0, 375, 64):
        n = min(64, 375 - start)
        spread = jnp.where(keep[None], turned[start : start + n][:, None, :], 0.0).astype(BF16)
        value = jnp.dot(spread.reshape(n * ROWS, 256), weights[...], preferred_element_type=F32)
        out_ref[start : start + n] = value.astype(BF16).reshape(n, ROWS, 128)

    pltpu.make_async_copy(lagall, lagall, lag_sem).wait()
    lag_ref[...] = jnp.sum(lagall[...], axis=0)[0:2, 0:16]

    sent = 28 + jnp.where(zl < NZ - 1, zl + 1, 0) + jnp.where(zl > 0, NZ - zl, 0)

    def left_block(t, carry):
        block(0, 0, 0, sibling).wait_send()
        return carry

    lax.fori_loop(0, sent, left_block, 0)

    def left_y(t, carry):
        over_y(0, 1).wait_send()
        gather_y(0, 1).wait_send()
        return carry

    lax.fori_loop(0, 12, left_y, 0)

    def left_own(t, carry):
        to_owner(1, 0).wait_send()
        return carry

    lax.fori_loop(0, 63, left_own, 0)

    def left_lag(t, carry):
        pltpu.make_async_remote_copy(
            src_ref=lagmine, dst_ref=lagall.at[pair], send_sem=send_lag, recv_sem=lag_sem,
            device_id=sibling, device_id_type=MESH,
        ).wait_send()
        return carry

    lax.fori_loop(0, 31, left_lag, 0)


def on_device(density, cholesky, virtual_orbitals, occupied_orbitals):
    anywhere = pl.BlockSpec(memory_space=pl.ANY)
    vmem = pl.BlockSpec(memory_space=pltpu.VMEM)
    dma = pltpu.SemaphoreType.DMA
    back, lagrangian = pl.pallas_call(
        kernel,
        name="density",
        out_shape=(jax.ShapeDtypeStruct((375, ROWS, 128), BF16), jax.ShapeDtypeStruct((2, 16), F32)),
        in_specs=[anywhere] * 4,
        out_specs=(vmem, vmem),
        scratch_shapes=[
            pltpu.VMEM((4, 8, ROWS, 3600), BF16),
            pltpu.VMEM((900, 3600), BF16),
            pltpu.VMEM((1800, 375), BF16),
            pltpu.VMEM((16, 128), F32),
            pltpu.VMEM((8, WIDE, 375), BF16),
            pltpu.VMEM((2, 8, ROWS, WIDE), F32),
            pltpu.VMEM((256, 128), BF16),
            pltpu.VMEM((4, NY, 128, WIDE), BF16),
            pltpu.VMEM((4, NY - 1, 128, WIDE), BF16),
            pltpu.VMEM((4, 8, ROWS, WIDE), BF16),
            pltpu.VMEM((4, 2, 8, ROWS, WIDE), BF16),
            pltpu.VMEM((4, NY, 8, ROWS, WIDE), BF16),
            pltpu.VMEM((4, 64, 375), F32),
            pltpu.VMEM((2, 16, 128), F32),
            pltpu.VMEM((8, 128), F32),
            pltpu.VMEM((32, 8, 128), F32),
            dma((3,)),
            dma,
            dma((4, 8)),
            dma((4, NY - 1)),
            dma((4,)),
            dma((4, NY - 1)),
            dma,
            dma,
            dma,
            dma,
            dma,
            dma,
        ],
        compiler_params=pltpu.CompilerParams(collective_id=0, has_side_effects=True, vmem_limit_bytes=56 * 2**20),
        cost_estimate=pl.CostEstimate(flops=5 * 10**9, bytes_accessed=12 * 2**20, transcendentals=0),
    )(density.T, cholesky, virtual_orbitals.T, occupied_orbitals.T.astype(F32))
    return back.transpose(1, 2, 0), lagrangian.T


def solution(mesh):
    return jax.shard_map(
        on_device,
        mesh=mesh,
        in_specs=(P("aux", "pair"), P("pair", "aux"), P("aux", None), P()),
        out_specs=(P("pair", None, "aux"), P(None, "aux")),
        check_vma=False,
    )
```

time: 317 us -> 77.2 us (0.24)
  blocking collectives: 167 us -> 0 us
  waiting for transfers between devices: 96.5 us -> 0 us
  Pallas kernels: 0 us -> 71.7 us
  starting transfers between devices: 21 us -> 0 us
  matrix products: 13.5 us -> 0 us
  between operations: 14.1 us -> 0.65 us
    psum x2 -> x0, blocking collectives: 167 us -> none  [the longest x1 99.6 us: on_device(): summed = lax.psum(partial_value, 'aux')]
    pallas_call x0 -> x1, Pallas kernels: none -> 71.7 us  [on_device(): pl.pallas_call(kernel, name='density', out_shape=(jax.ShapeDtypeStruct((3...]
    all_gather x1 -> x0, waiting for transfers between devices: 68.7 us -> none  [on_device(): lax.all_gather(cholesky, 'pair', axis=0, tiled=True)]
    all_to_all x1 -> x0, waiting for transfers between devices: 27.1 us -> none  [on_device(): lax.all_to_all(summed.astype(jnp.bfloat16), 'pair', split_axis=0, concat_...]
    all_to_all x1 -> x0, starting transfers between devices: 21 us -> none  [on_device(): lax.all_to_all(summed.astype(jnp.bfloat16), 'pair', split_axis=0, concat_...]
    dot_general x3 -> x0, matrix products: 13.5 us -> none  [the longest x1 9.11 us: on_device(): jnp.dot(lax.all_gather(cholesky, 'pair', axis=0, tiled=True), density, pr...]
  transfers between devices with their start and end apart: 2 -> 0, of which waited for: 2 -> 0; matrix products, arithmetic and copies ran while one was open for 0% -> 0% of each run, Pallas kernels for 0% -> 0%
where the time goes in v1:
time: 77.2 us; the launch traced here: 77 us
  Pallas kernels  71.7 us (93%)
  local copies, waits for them, and re-layouts  3.36 us (4%)
  other arithmetic  1.29 us (2%)
    pallas_call x1, Pallas kernels, on_device(): pl.pallas_call(kernel, name='density', out_shape=(jax.ShapeDtypeStruct((3...  71.7 us
    unnamed x4, local copies, waits for them, and re-layouts  3.36 us

profile of v1, /device:TPU:1, one launch (start us, length us, event | category | flops | bytes accessed | tf_op | source)
XLA Modules:
  0.0 77.0 jit_solution(14019040340633612100)
XLA Ops:
  0.6 1.3 %convert_bitcast_fusion.occ_hbm = f32[16,128]{1,0:T(8,128)} fusion(bf16[128,16]{0,1:T(8,128)(2,1)} %param.7), kind=kLoop, calls=%fused_computation | loop fusion | flops 2048 | bytes 12288 | tf_op jit(solution)/shard_map/convert_element_type | solution.py:364
  1.9 71.7 %density.1 = (bf16[375,16,128]{2,1,0:T(8,128)(2,1)}, f32[2,16]{1,0:T(2,128)}) custom-call(bf16[900,3600]{1,0:T(8,128)(2,1)} %bitcast.8, bf16[16,3600]{1,0:T(8,128)(2,1)} %chol_hbm.1, bf16[1800,375]{1,0:T(8,128)(2,1)} %bitcast.9, f32[16,128]{1,0:T(8,128)} %convert_bitcast_fusion.occ_hbm), custom_call_target="tpu_custom_call" | custom-call | flops 5000000000 | bytes 12582912 | tf_op jit(solution)/shard_map/density/pallas_call | solution.py:326
  73.7 0.0 copy-start
  73.7 2.8 %copy.8 = bf16[16,128,375]{1,0,2:T(8,128)(2,1)} copy(bf16[16,128,375]{1,0,2:T(8,128)(2,1)} %bitcast.6) | data formatting | bytes 3072000
  76.5 0.0 copy-done
  76.5 0.6 copy.9
Async XLA Ops:
  73.7 2.8 %copy-start = (f32[2,16]{1,0:T(2,128)S(1)}, f32[2,16]{1,0:T(2,128)}, u32[]{:S(2)}) copy-start(f32[2,16]{1,0:T(2,128)} %get-tuple-element.5) | copy-start | bytes 388

commit v2 on v0

v2 whole, which is shorter than its diff:
```python
import jax
import jax.numpy as jnp
from jax import lax
from jax.experimental import pallas as pl
from jax.experimental.pallas import tpu as pltpu
from jax.sharding import PartitionSpec as P

MESH = pl.DeviceIdType.MESH
F32 = jnp.float32
BF16 = jnp.bfloat16
NT = (((1,), (1,)), ((), ()))

NX, NY, NZ, NC = 4, 4, 4, 2
ROWS = 16
CUT = 224
LAST = 228
WIDE = 256
HALVES = (0, 1792, 3600)
NCHOL = 512


def kernel(
    dt_hbm, chol_hbm, virt_hbm, occ_hbm, out_ref, lag_ref,
    gath, dt, virt, occ, occ32, virtp, lc, weights, part, mine, fromy, summed, owned, gamma, turned, lagrow, lagmine, lagall,
    local_sem, bulk_sem, block_sem, y_sem, own_sem, g_sem, lag_sem, plane_sem,
    send_first, send_second, send_y, send_own, send_g, send_lag,
):
    aux, pair = lax.axis_index("aux"), lax.axis_index("pair")
    zh, y = aux // NY, aux % NY
    x, zl, c = pair // (NZ * NC), (pair // NC) % NZ, pair % NC
    me = c * NX + x
    rows_of = (zl, zl + 1 - 2 * lax.rem(zl, 2), lax.rem(zl + 2, NZ), NZ - 1 - zl)

    auxes = [[(zh * NY if d == 0 else (1 - zh) * NY) + lax.rem(y + e, NY) for e in range(NY)] for d in range(2)]
    xs = [lax.rem(x + d, NX) for d in range(NX)]
    zs = [lax.rem(zl + d, NZ) for d in range(NZ)]
    cs = [c, 1 - c]

    def device(dzh=0, dy=0, dx=0, dz=0, dc=0):
        return (auxes[dzh][dy], (xs[dx] * NZ + zs[dz]) * NC + cs[dc])

    right, left, sibling, up, down = device(dx=1), device(dx=3), device(dc=1), device(dz=1), device(dz=3)
    across = device(dzh=1)

    barrier = pltpu.get_barrier_semaphore()
    friends = [right, left, sibling, up, down, across] + [device(dy=e) for e in range(1, NY)]
    for friend in friends:
        pl.semaphore_signal(barrier, inc=1, device_id=friend, device_id_type=MESH)

    own = pltpu.make_async_copy(chol_hbm, gath.at[0, c * NX], local_sem.at[0])
    own.start()
    load_occ = pltpu.make_async_copy(occ_hbm, occ, local_sem.at[2])
    load_occ.start()
    load_virt = pltpu.make_async_copy(virt_hbm, virt, local_sem.at[1])
    load_virt.start()
    load_dt = pltpu.make_async_copy(dt_hbm, dt, bulk_sem)
    load_dt.start()

    def block(src, dst, h, target):
        cols = pl.ds(HALVES[h], HALVES[h + 1] - HALVES[h])
        return pltpu.make_async_remote_copy(
            src_ref=gath.at[src[0], src[1], :, cols], dst_ref=gath.at[dst[0], dst[1], :, cols],
            send_sem=(send_first, send_second)[h], recv_sem=block_sem.at[h, dst[0], dst[1]],
            device_id=target, device_id_type=MESH,
        )

    def arrived(q, j, h):
        block((q, j), (q, j), h, sibling).wait_recv()

    def xor(a, b):
        return a + b - 2 * (lax.rem(a, 2) * lax.rem(b, 2)) - 4 * ((a // 2) * (b // 2))

    mine_first = c * NX

    def along_z(s_, h):
        above, below = zl + s_, zl - s_

        @pl.when(above < NZ)
        def _():
            at = xor(zl, above)
            if s_ > 0:
                arrived(at, mine_first, h)

            @pl.when(zl > 0)
            def _():
                block((at, mine_first), (xor(zl - 1, above), mine_first), h, down).start()

        @pl.when(below >= 0)
        def _():
            at = xor(zl, below)
            if s_ > 0:
                arrived(at, mine_first, h)

            @pl.when(zl < NZ - 1)
            def _():
                block((at, mine_first), (xor(zl + 1, below), mine_first), h, up).start()

    def own_column(q, h):
        along_z(q, h)
        block((q, mine_first), (q, mine_first + 3), h, right).start()
        block((q, mine_first), (q, mine_first + 1), h, left).start()
        block((q, mine_first), (q, mine_first), h, sibling).start()

    def beside(q, h):
        for g, other, target in ((1, 0, left), (3, 1, right)):
            j = mine_first + g
            arrived(q, j, h)
            if q % 2 == 1 - other:
                block((q, j), (q, mine_first + 2), h, target).start()
            block((q, j), (q, j), h, sibling).start()

    def opposite(q):
        j = mine_first + 2
        for h in range(2):
            arrived(q, j, h)
            block((q, j), (q, j), h, sibling).start()

    def from_sibling(q):
        for g in range(NX):
            for h in range(2):
                arrived(q, (1 - c) * NX + g, h)
        pl.semaphore_signal(plane_sem.at[q], inc=1, device_id=across, device_id_type=MESH)

    def over_y(k, t):
        return pltpu.make_async_remote_copy(
            src_ref=part.at[k, t], dst_ref=fromy.at[k, t], send_sem=send_y, recv_sem=y_sem.at[k, t],
            device_id=device(dy=t + 1), device_id_type=MESH,
        )

    def product(k, t):
        rows = gath[k].reshape(128, 3600)
        cut = lax.rem(y + 1 + t, NY)
        pairs = dt[pl.ds(pl.multiple_of(cut * CUT, 16), LAST), :]
        value = lax.dot_general(rows, pairs, NT, preferred_element_type=F32)
        if t < NY - 1:
            part[k, t, :, 0:LAST] = value.astype(BF16)
            over_y(k, t).start()
        else:
            mine[k, :, 0:LAST] = value

    def to_owner(k, dzh, g, dc):
        return pltpu.make_async_remote_copy(
            src_ref=summed.at[k, cs[dc] * NX + g], dst_ref=owned.at[k, zh, me],
            send_sem=send_own, recv_sem=own_sem.at[k],
            device_id=(auxes[dzh][0], (xs[g] * NZ + rows_of[k]) * NC + cs[dc]), device_id_type=MESH,
        )

    def sum_y(k):
        total = mine[k]
        for t in range(NY - 1):
            over_y(k, t).wait_recv()
            total = total + fromy[k, t].astype(F32)
        summed[k] = total.astype(BF16).reshape(8, ROWS, WIDE)
        pl.semaphore_wait(plane_sem.at[k], 1)
        for dzh in (1, 0):
            for g in (2, 1, 3, 0):
                for dc in range(NC):
                    if k == 0 and g == 0 and dc == 0 and dzh == 0:
                        pltpu.make_async_copy(summed.at[k, c * NX], owned.at[0, zh, me], own_sem.at[0]).start()
                    else:
                        to_owner(k, dzh, g, dc).start()

    def gather_y(k, t):
        return pltpu.make_async_remote_copy(
            src_ref=gamma.at[k, y], dst_ref=gamma.at[k, y], send_sem=send_g, recv_sem=g_sem.at[k, t],
            device_id=device(dy=t + 1), device_id_type=MESH,
        )

    def complete(k):
        pltpu.make_async_copy(owned.at[k], owned.at[k], own_sem.at[k]).wait()
        gamma[k, y] = (owned[k, 0].astype(F32) + owned[k, 1].astype(F32)).astype(BF16)
        for t in range(NY - 1):
            gather_y(k, t).start()

    def transform(k):
        for t in range(NY - 1):
            gather_y(k, t).wait_recv()
        total = jnp.zeros((64, 375), F32)
        for h in range(2):
            for cut in range(NY):
                total = total + jnp.dot(
                    gamma[k, cut, pl.ds(4 * h, 4)].reshape(64, WIDE), virtp[4 * h + cut], preferred_element_type=F32
                )
        turned[:, k * 64 : (k + 1) * 64] = total.astype(BF16).astype(F32).T
        for z in range(NZ):
            i = z * NZ + rows_of[k]
            for j in range(2):
                terms = jnp.zeros((ROWS, WIDE), F32)
                for h in range(2):
                    for cut in range(NY):
                        terms = terms + gamma[k, cut, 4 * h + z].astype(F32) * lc[j, 4 * h + cut]
                terms = terms[:, :128] + terms[:, 128:]
                lagrow[j, pl.ds(i, 1), :] = jnp.sum(terms, axis=0, keepdims=True)

    def pad_virtual(h):
        for cut in range(NY):
            width = LAST if cut == NY - 1 else CUT
            start = h * 900 + cut * CUT
            first = start // 8 * 8
            value = virt[first : start + width, :].astype(F32)
            virtp[4 * h + cut, 0:width, :] = value[start - first :].astype(BF16)

    own.wait()
    virtp[...] = jnp.zeros(virtp.shape, BF16)
    pl.semaphore_wait(barrier, len(friends))
    own_column(0, 0)
    own_column(0, 1)

    part[:, :, :, 128:WIDE] = jnp.zeros((4, NY - 1, 128, WIDE - 128), BF16)
    mine[:, :, 128:WIDE] = jnp.zeros((4, 128, WIDE - 128), F32)
    lc[...] = jnp.zeros(lc.shape, F32)
    lagmine[...] = jnp.zeros(lagmine.shape, F32)
    load_occ.wait()
    occ32[...] = occ[...].astype(F32)
    for k in range(4):
        for z in range(NZ):
            row = occ32[pl.ds(z * NZ + rows_of[k], 1), :]
            weights[pl.ds(k * 64 + z * 16, 16), :] = jnp.broadcast_to(row, (16, 128)).astype(BF16)

    own_column(1, 0)
    beside(0, 0)
    own_column(1, 1)
    beside(0, 1)
    load_virt.wait()
    pad_virtual(0)
    own_column(2, 0)
    own_column(2, 1)
    opposite(0)
    beside(1, 0)
    beside(1, 1)
    pad_virtual(1)
    own_column(3, 0)
    own_column(3, 1)
    own_block = gath[0, c * NX].astype(F32)
    for j in range(2):
        for h in range(2):
            for cut in range(NY):
                width = LAST if cut == NY - 1 else CUT
                start = j * 1800 + h * 900 + cut * CUT
                lc[j, 4 * h + cut, :, 0:width] = own_block[:, start : start + width]
    from_sibling(0)
    load_dt.wait()
    product(0, 0)
    beside(2, 0)
    product(0, 1)
    beside(2, 1)
    product(0, 2)
    opposite(1)
    product(0, 3)
    beside(3, 0)
    from_sibling(1)
    product(1, 0)
    beside(3, 1)
    product(1, 1)
    product(1, 2)
    opposite(2)
    product(1, 3)
    sum_y(0)
    from_sibling(2)
    product(2, 0)
    product(2, 1)
    opposite(3)
    product(2, 2)
    product(2, 3)
    sum_y(1)
    from_sibling(3)
    for t in range(NY):
        product(3, t)
    complete(0)
    sum_y(2)
    complete(1)
    sum_y(3)
    transform(0)
    complete(2)
    transform(1)
    transform(2)
    complete(3)
    transform(3)

    lagmine[0:2, 0:16] = jnp.sum(lagrow[...], axis=-1) * (1.0 / NCHOL)

    def share(t):
        return pltpu.make_async_remote_copy(
            src_ref=lagmine, dst_ref=lagall.at[pair], send_sem=send_lag, recv_sem=lag_sem,
            device_id=(aux, lax.rem(pair + t, 32)), device_id_type=MESH,
        )

    def start_share(t, carry):
        share(t).start()
        return carry

    pltpu.make_async_copy(lagmine, lagall.at[pair], lag_sem).start()
    lax.fori_loop(1, 32, start_share, 0)

    row = lax.broadcasted_iota(jnp.int32, (ROWS, 256), 0)
    lane = lax.broadcasted_iota(jnp.int32, (ROWS, 256), 1)
    keep = (lane % ROWS) == row
    for start in range(0, 375, 64):
        n = min(64, 375 - start)
        spread = jnp.where(keep[None], turned[start : start + n][:, None, :], 0.0).astype(BF16)
        value = jnp.dot(spread.reshape(n * ROWS, 256), weights[...], preferred_element_type=F32)
        out_ref[start : start + n] = value.astype(BF16).reshape(n, ROWS, 128)

    pltpu.make_async_copy(lagall, lagall, lag_sem).wait()
    lag_ref[...] = jnp.sum(lagall[...], axis=0)[0:2, 0:16]

    sent = 28 + jnp.where(zl < NZ - 1, zl + 1, 0) + jnp.where(zl > 0, NZ - zl, 0)

    def left_block(t, carry):
        block((0, 0), (0, 0), 0, sibling).wait_send()
        block((0, 0), (0, 0), 1, sibling).wait_send()
        return carry

    def left_y(t, carry):
        over_y(0, 0).wait_send()
        gather_y(0, 0).wait_send()
        return carry

    def left_own(t, carry):
        to_owner(1, 0, 0, 0).wait_send()
        return carry

    def left_lag(t, carry):
        share(1).wait_send()
        return carry

    lax.fori_loop(0, sent, left_block, 0)
    lax.fori_loop(0, 12, left_y, 0)
    lax.fori_loop(0, 63, left_own, 0)
    lax.fori_loop(0, 31, left_lag, 0)


def on_device(density, cholesky, virtual_orbitals, occupied_orbitals):
    hbm = pl.BlockSpec(memory_space=pltpu.HBM)
    vmem = pl.BlockSpec(memory_space=pltpu.VMEM)
    dma = pltpu.SemaphoreType.DMA
    back, lagrangian = pl.pallas_call(
        kernel,
        name="density",
        out_shape=(jax.ShapeDtypeStruct((375, ROWS, 128), BF16), jax.ShapeDtypeStruct((2, 16), F32)),
        in_specs=[hbm] * 4,
        out_specs=(vmem, vmem),
        scratch_shapes=[
            pltpu.VMEM((4, 8, ROWS, 3600), BF16),
            pltpu.VMEM((900, 3600), BF16),
            pltpu.VMEM((1800, 375), BF16),
            pltpu.VMEM((16, 128), BF16),
            pltpu.VMEM((16, 128), F32),
            pltpu.VMEM((8, WIDE, 375), BF16),
            pltpu.VMEM((2, 8, ROWS, WIDE), F32),
            pltpu.VMEM((256, 128), BF16),
            pltpu.VMEM((4, NY - 1, 128, WIDE), BF16),
            pltpu.VMEM((4, 128, WIDE), F32),
            pltpu.VMEM((4, NY - 1, 128, WIDE), BF16),
            pltpu.VMEM((4, 8, ROWS, WIDE), BF16),
            pltpu.VMEM((4, 2, 8, ROWS, WIDE), BF16),
            pltpu.VMEM((4, NY, 8, ROWS, WIDE), BF16),
            pltpu.VMEM((375, 256), F32),
            pltpu.VMEM((2, 16, 128), F32),
            pltpu.VMEM((2, 128), F32),
            pltpu.VMEM((32, 2, 128), F32),
            dma((3,)),
            dma,
            dma((2, 4, 8)),
            dma((4, NY - 1)),
            dma((4,)),
            dma((4, NY - 1)),
            dma,
            pltpu.SemaphoreType.REGULAR((4,)),
            dma,
            dma,
            dma,
            dma,
            dma,
            dma,
        ],
        compiler_params=pltpu.CompilerParams(collective_id=0, has_side_effects=True, vmem_limit_bytes=58 * 2**20),
        cost_estimate=pl.CostEstimate(flops=5 * 10**9, bytes_accessed=12 * 2**20, transcendentals=0),
    )(density.T, cholesky, virtual_orbitals.T, occupied_orbitals.T)
    return back.transpose(1, 2, 0), lagrangian.T


def solution(mesh):
    return jax.shard_map(
        on_device,
        mesh=mesh,
        in_specs=(P("aux", "pair"), P("pair", "aux"), P("aux", None), P()),
        out_specs=(P("pair", None, "aux"), P(None, "aux")),
        check_vma=False,
    )
```

time: 317 us -> 71.5 us (0.23)
  blocking collectives: 167 us -> 0 us
  waiting for transfers between devices: 96.5 us -> 0 us
  Pallas kernels: 0 us -> 67.4 us
  starting transfers between devices: 21 us -> 0 us
  matrix products: 13.5 us -> 0 us
  between operations: 14.1 us -> 0.65 us
    psum x2 -> x0, blocking collectives: 167 us -> none  [the longest x1 99.6 us: on_device(): summed = lax.psum(partial_value, 'aux')]
    all_gather x1 -> x0, waiting for transfers between devices: 68.7 us -> none  [on_device(): lax.all_gather(cholesky, 'pair', axis=0, tiled=True)]
    pallas_call x0 -> x1, Pallas kernels: none -> 67.4 us  [on_device(): pl.pallas_call(kernel, name='density', out_shape=(jax.ShapeDtypeStruct((3...]
    all_to_all x1 -> x0, waiting for transfers between devices: 27.1 us -> none  [on_device(): lax.all_to_all(summed.astype(jnp.bfloat16), 'pair', split_axis=0, concat_...]
    all_to_all x1 -> x0, starting transfers between devices: 21 us -> none  [on_device(): lax.all_to_all(summed.astype(jnp.bfloat16), 'pair', split_axis=0, concat_...]
    dot_general x3 -> x0, matrix products: 13.5 us -> none  [the longest x1 9.11 us: on_device(): jnp.dot(lax.all_gather(cholesky, 'pair', axis=0, tiled=True), density, pr...]
  transfers between devices with their start and end apart: 2 -> 0, of which waited for: 2 -> 0; matrix products, arithmetic and copies ran while one was open for 0% -> 0% of each run, Pallas kernels for 0% -> 0%
where the time goes in v2:
time: 71.5 us; the launch traced here: 71.4 us
  Pallas kernels  67.4 us (94%)
  local copies, waits for them, and re-layouts  3.36 us (5%)
    pallas_call x1, Pallas kernels, on_device(): pl.pallas_call(kernel, name='density', out_shape=(jax.ShapeDtypeStruct((3...  67.4 us
    unnamed x4, local copies, waits for them, and re-layouts  3.36 us

profile of v2, /device:TPU:1, one launch (start us, length us, event | category | flops | bytes accessed | tf_op | source)
XLA Modules:
  0.0 71.4 jit_solution(11435931489146396588)
XLA Ops:
  0.6 67.4 %density.1 = (bf16[375,16,128]{2,1,0:T(8,128)(2,1)}, f32[2,16]{1,0:T(2,128)}) custom-call(bf16[900,3600]{1,0:T(8,128)(2,1)} %bitcast.7, bf16[16,3600]{1,0:T(8,128)(2,1)} %chol_hbm.1, bf16[1800,375]{1,0:T(8,128)(2,1)} %bitcast.8, bf16[16,128]{1,0:T(8,128)(2,1)} %bitcast.9), custom_call_target="tpu_custom_call" | custom-call | flops 5000000000 | bytes 12582912 | tf_op jit(solution)/shard_map/density/pallas_call | solution.py:337
  68.0 0.0 copy-start
  68.1 2.8 %copy.8 = bf16[16,128,375]{1,0,2:T(8,128)(2,1)} copy(bf16[16,128,375]{1,0,2:T(8,128)(2,1)} %bitcast.5) | data formatting | bytes 3072000
  70.8 0.0 copy-done
  70.8 0.6 copy.9
Async XLA Ops:
  68.0 2.8 %copy-start = (f32[2,16]{1,0:T(2,128)S(1)}, f32[2,16]{1,0:T(2,128)}, u32[]{:S(2)}) copy-start(f32[2,16]{1,0:T(2,128)} %get-tuple-element.5) | copy-start | bytes 388

commit v3 on v2

--- a/solution.py
+++ b/solution.py
@@ -20,8 +20,8 @@
 
 
 def kernel(
-    dt_hbm, chol_hbm, virt_hbm, occ_hbm, out_ref, lag_ref,
-    gath, dt, virt, occ, occ32, virtp, lc, weights, part, mine, fromy, summed, owned, gamma, turned, lagrow, lagmine, lagall,
+    dt_hbm, chol_hbm, virt_hbm, occ_hbm, turned, weights, lag_ref,
+    gath, dt, virt, occ, occ32, virtp, lc, part, mine, fromy, summed, owned, gamma, lagrow, lagmine, lagall,
     local_sem, bulk_sem, block_sem, y_sem, own_sem, g_sem, lag_sem, plane_sem,
     send_first, send_second, send_y, send_own, send_g, send_lag,
 ):
@@ -172,9 +172,11 @@
         for t in range(NY - 1):
             gather_y(k, t).start()
 
-    def transform(k):
+    def here(k):
         for t in range(NY - 1):
             gather_y(k, t).wait_recv()
+
+    def half_done(k):
         total = jnp.zeros((64, 375), F32)
         for h in range(2):
             for cut in range(NY):
@@ -182,6 +184,8 @@
                     gamma[k, cut, pl.ds(4 * h, 4)].reshape(64, WIDE), virtp[4 * h + cut], preferred_element_type=F32
                 )
         turned[:, k * 64 : (k + 1) * 64] = total.astype(BF16).astype(F32).T
+
+    def lagrangian(k):
         for z in range(NZ):
             i = z * NZ + rows_of[k]
             for j in range(2):
@@ -206,8 +210,12 @@
     own_column(0, 0)
     own_column(0, 1)
 
+    own_column(1, 0)
+    beside(0, 0)
     part[:, :, :, 128:WIDE] = jnp.zeros((4, NY - 1, 128, WIDE - 128), BF16)
     mine[:, :, 128:WIDE] = jnp.zeros((4, 128, WIDE - 128), F32)
+    own_column(1, 1)
+    beside(0, 1)
     lc[...] = jnp.zeros(lc.shape, F32)
     lagmine[...] = jnp.zeros(lagmine.shape, F32)
     load_occ.wait()
@@ -216,19 +224,14 @@
         for z in range(NZ):
             row = occ32[pl.ds(z * NZ + rows_of[k], 1), :]
             weights[pl.ds(k * 64 + z * 16, 16), :] = jnp.broadcast_to(row, (16, 128)).astype(BF16)
-
-    own_column(1, 0)
-    beside(0, 0)
-    own_column(1, 1)
-    beside(0, 1)
+    own_column(2, 0)
     load_virt.wait()
     pad_virtual(0)
-    own_column(2, 0)
     own_column(2, 1)
     opposite(0)
     beside(1, 0)
+    pad_virtual(1)
     beside(1, 1)
-    pad_virtual(1)
     own_column(3, 0)
     own_column(3, 1)
     own_block = gath[0, c * NX].astype(F32)
@@ -266,16 +269,18 @@
     from_sibling(3)
     for t in range(NY):
         product(3, t)
+    sum_y(2)
     complete(0)
-    sum_y(2)
+    sum_y(3)
     complete(1)
-    sum_y(3)
-    transform(0)
     complete(2)
-    transform(1)
-    transform(2)
     complete(3)
-    transform(3)
+    for k in range(3):
+        here(k)
+        lagrangian(k)
+    half_done(0)
+    here(3)
+    lagrangian(3)
 
     lagmine[0:2, 0:16] = jnp.sum(lagrow[...], axis=-1) * (1.0 / NCHOL)
 
@@ -292,54 +297,69 @@
     pltpu.make_async_copy(lagmine, lagall.at[pair], lag_sem).start()
     lax.fori_loop(1, 32, start_share, 0)
 
+    for k in range(1, 4):
+        half_done(k)
+    pltpu.make_async_copy(lagall, lagall, lag_sem).wait()
+    lag_ref[...] = jnp.sum(lagall[...], axis=0)[0:2, 0:16]
+
+    sent = 28 + jnp.where(zl < NZ - 1, zl + 1, 0) + jnp.where(zl > 0, NZ - zl, 0)
+
+    def left_block(t, carry):
+        block((0, 0), (0, 0), 0, sibling).wait_send()
+        block((0, 0), (0, 0), 1, sibling).wait_send()
+        return carry
+
+    def left_y(t, carry):
+        over_y(0, 0).wait_send()
+        gather_y(0, 0).wait_send()
+        return carry
+
+    def left_own(t, carry):
+        to_owner(1, 0, 0, 0).wait_send()
+        return carry
+
+    def left_lag(t, carry):
+        share(1).wait_send()
+        return carry
+
+    lax.fori_loop(0, sent, left_block, 0)
+    lax.fori_loop(0, 12, left_y, 0)
+    lax.fori_loop(0, 63, left_own, 0)
+    lax.fori_loop(0, 31, left_lag, 0)
+
+
+def second(turned, weights, terms, out_hbm, lag_ref, out, sem):
     row = lax.broadcasted_iota(jnp.int32, (ROWS, 256), 0)
     lane = lax.broadcasted_iota(jnp.int32, (ROWS, 256), 1)
     keep = (lane % ROWS) == row
+    copies = []
     for start in range(0, 375, 64):
         n = min(64, 375 - start)
         spread = jnp.where(keep[None], turned[start : start + n][:, None, :], 0.0).astype(BF16)
         value = jnp.dot(spread.reshape(n * ROWS, 256), weights[...], preferred_element_type=F32)
-        out_ref[start : start + n] = value.astype(BF16).reshape(n, ROWS, 128)
-
-    pltpu.make_async_copy(lagall, lagall, lag_sem).wait()
-    lag_ref[...] = jnp.sum(lagall[...], axis=0)[0:2, 0:16]
-
-    sent = 28 + jnp.where(zl < NZ - 1, zl + 1, 0) + jnp.where(zl > 0, NZ - zl, 0)
-
-    def left_block(t, carry):
-        block((0, 0), (0, 0), 0, sibling).wait_send()
-        block((0, 0), (0, 0), 1, sibling).wait_send()
-        return carry
-
-    def left_y(t, carry):
-        over_y(0, 0).wait_send()
-        gather_y(0, 0).wait_send()
-        return carry
-
-    def left_own(t, carry):
-        to_owner(1, 0, 0, 0).wait_send()
-        return carry
-
-    def left_lag(t, carry):
-        share(1).wait_send()
-        return carry
-
-    lax.fori_loop(0, sent, left_block, 0)
-    lax.fori_loop(0, 12, left_y, 0)
-    lax.fori_loop(0, 63, left_own, 0)
-    lax.fori_loop(0, 31, left_lag, 0)
+        out[start : start + n] = value.astype(BF16).reshape(n, ROWS, 128)
+        rows = pl.ds(start, n)
+        copies.append(pltpu.make_async_copy(out.at[rows], out_hbm.at[rows], sem.at[start // 64]))
+        copies[-1].start()
+    lag_ref[...] = terms[...]
+    for copy in copies:
+        copy.wait()
 
 
 def on_device(density, cholesky, virtual_orbitals, occupied_orbitals):
     hbm = pl.BlockSpec(memory_space=pltpu.HBM)
     vmem = pl.BlockSpec(memory_space=pltpu.VMEM)
     dma = pltpu.SemaphoreType.DMA
-    back, lagrangian = pl.pallas_call(
+    turned, weights, terms = pl.pallas_call(
         kernel,
         name="density",
-        out_shape=(jax.ShapeDtypeStruct((375, ROWS, 128), BF16), jax.ShapeDtypeStruct((2, 16), F32)),
+        out_shape=(
+            jax.ShapeDtypeStruct((375, 256), F32),
+            jax.ShapeDtypeStruct((256, 128), BF16),
+            jax.ShapeDtypeStruct((2, 16), F32),
+        ),
         in_specs=[hbm] * 4,
-        out_specs=(vmem, vmem),
+        out_specs=(vmem, vmem, vmem),
         scratch_shapes=[
             pltpu.VMEM((4, 8, ROWS, 3600), BF16),
             pltpu.VMEM((900, 3600), BF16),
@@ -348,14 +368,12 @@
             pltpu.VMEM((16, 128), F32),
             pltpu.VMEM((8, WIDE, 375), BF16),
             pltpu.VMEM((2, 8, ROWS, WIDE), F32),
-            pltpu.VMEM((256, 128), BF16),
             pltpu.VMEM((4, NY - 1, 128, WIDE), BF16),
             pltpu.VMEM((4, 128, WIDE), F32),
             pltpu.VMEM((4, NY - 1, 128, WIDE), BF16),
             pltpu.VMEM((4, 8, ROWS, WIDE), BF16),
             pltpu.VMEM((4, 2, 8, ROWS, WIDE), BF16),
             pltpu.VMEM((4, NY, 8, ROWS, WIDE), BF16),
-            pltpu.VMEM((375, 256), F32),
             pltpu.VMEM((2, 16, 128), F32),
             pltpu.VMEM((2, 128), F32),
             pltpu.VMEM((32, 2, 128), F32),
@@ -377,6 +395,16 @@
         compiler_params=pltpu.CompilerParams(collective_id=0, has_side_effects=True, vmem_limit_bytes=58 * 2**20),
         cost_estimate=pl.CostEstimate(flops=5 * 10**9, bytes_accessed=12 * 2**20, transcendentals=0),
     )(density.T, cholesky, virtual_orbitals.T, occupied_orbitals.T)
+    back, lagrangian = pl.pallas_call(
+        second,
+        name="second",
+        out_shape=(jax.ShapeDtypeStruct((375, ROWS, 128), BF16), jax.ShapeDtypeStruct((2, 16), F32)),
+        in_specs=[vmem] * 3,
+        out_specs=(hbm, vmem),
+        scratch_shapes=[pltpu.VMEM((375, ROWS, 128), BF16), dma((6,))],
+        compiler_params=pltpu.CompilerParams(vmem_limit_bytes=60 * 2**20),
+        cost_estimate=pl.CostEstimate(flops=4 * 10**8, bytes_accessed=2 * 2**20, transcendentals=0),
+    )(turned, weights, terms)
     return back.transpose(1, 2, 0), lagrangian.T
 
 

time: 71.5 us -> 69.2 us (0.968)
  local copies, waits for them, and re-layouts: 3.36 us -> 0 us
  Pallas kernels: 67.4 us -> 68.4 us
    pallas_call x0 -> x1, Pallas kernels: none -> 3.47 us  [on_device(): pl.pallas_call(second, name='second', out_shape=(jax.ShapeDtypeStruct((37...]
    unnamed x4 -> x0, local copies, waits for them, and re-layouts: 3.36 us -> none
    pallas_call x1, Pallas kernels: 67.4 us -> 65 us  [on_device(): pl.pallas_call(kernel, name='density', out_shape=(jax.ShapeDtypeStruct((3...]
where the time goes in v3:
time: 69.2 us; the launch traced here: 69.1 us
  Pallas kernels  68.4 us (99%)
    pallas_call x1, Pallas kernels, on_device(): pl.pallas_call(kernel, name='density', out_shape=(jax.ShapeDtypeStruct((3...  65 us
    pallas_call x1, Pallas kernels, on_device(): pl.pallas_call(second, name='second', out_shape=(jax.ShapeDtypeStruct((37...  3.47 us

profile of v3, /device:TPU:1, one launch (start us, length us, event | category | flops | bytes accessed | tf_op | source)
XLA Modules:
  0.0 69.1 jit_solution(15723080166399494052)
XLA Ops:
  0.6 65.0 %density.1 = (f32[375,256]{1,0:T(8,128)}, bf16[256,128]{1,0:T(8,128)(2,1)}, f32[2,16]{1,0:T(2,128)}) custom-call(bf16[900,3600]{1,0:T(8,128)(2,1)} %bitcast.5, bf16[16,3600]{1,0:T(8,128)(2,1)} %chol_hbm.1, bf16[1800,375]{1,0:T(8,128)(2,1)} %bitcast.6, bf16[16,128]{1,0:T(8,128)(2,1)} %bitcast.7), custom_call_target="tpu_custom_call" | custom-call | flops 5000000000 | bytes 12582912 | tf_op jit(solution)/shard_map/density/pallas_call | solution.py:353
  65.6 3.5 %second.1 = (bf16[375,16,128]{2,1,0:T(8,128)(2,1)}, f32[2,16]{1,0:T(2,128)}) custom-call(f32[375,256]{1,0:T(8,128)} %get-tuple-element.7.turned, bf16[256,128]{1,0:T(8,128)(2,1)} %get-tuple-element.8.weights, f32[2,16]{1,0:T(2,128)} %get-tuple-element.9.terms), custom_call_target="tpu_custom_call" | custom-call | flops 400000000 | bytes 2097152 | tf_op jit(solution)/shard_map/second/pallas_call | solution.py:398

commit v4 on v3

--- a/solution.py
+++ b/solution.py
@@ -267,9 +267,11 @@
     product(2, 3)
     sum_y(1)
     from_sibling(3)
-    for t in range(NY):
-        product(3, t)
+    product(3, 0)
+    product(3, 1)
     sum_y(2)
+    product(3, 2)
+    product(3, 3)
     complete(0)
     sum_y(3)
     complete(1)

time: 69.2 us -> 68.3 us (0.987)
  Pallas kernels: 68.4 us -> 67.5 us
    pallas_call x1, Pallas kernels: 65 us -> 64.1 us  [on_device(): pl.pallas_call(kernel, name='density', out_shape=(jax.ShapeDtypeStruct((3...]
where the time goes in v4:
time: 68.3 us; the launch traced here: 68.2 us
  Pallas kernels  67.5 us (99%)
    pallas_call x1, Pallas kernels, on_device(): pl.pallas_call(kernel, name='density', out_shape=(jax.ShapeDtypeStruct((3...  64.1 us
    pallas_call x1, Pallas kernels, on_device(): pl.pallas_call(second, name='second', out_shape=(jax.ShapeDtypeStruct((37...  3.47 us

profile of v4, /device:TPU:1, one launch (start us, length us, event | category | flops | bytes accessed | tf_op | source)
XLA Modules:
  0.0 68.2 jit_solution(7757560144873847387)
XLA Ops:
  0.6 64.1 %density.1 = (f32[375,256]{1,0:T(8,128)}, bf16[256,128]{1,0:T(8,128)(2,1)}, f32[2,16]{1,0:T(2,128)}) custom-call(bf16[900,3600]{1,0:T(8,128)(2,1)} %bitcast.5, bf16[16,3600]{1,0:T(8,128)(2,1)} %chol_hbm.1, bf16[1800,375]{1,0:T(8,128)(2,1)} %bitcast.6, bf16[16,128]{1,0:T(8,128)(2,1)} %bitcast.7), custom_call_target="tpu_custom_call" | custom-call | flops 5000000000 | bytes 12582912 | tf_op jit(solution)/shard_map/density/pallas_call | solution.py:355
  64.7 3.5 %second.1 = (bf16[375,16,128]{2,1,0:T(8,128)(2,1)}, f32[2,16]{1,0:T(2,128)}) custom-call(f32[375,256]{1,0:T(8,128)} %get-tuple-element.7.turned, bf16[256,128]{1,0:T(8,128)(2,1)} %get-tuple-element.8.weights, f32[2,16]{1,0:T(2,128)} %get-tuple-element.9.terms), custom_call_target="tpu_custom_call" | custom-call | flops 400000000 | bytes 2097152 | tf_op jit(solution)/shard_map/second/pallas_call | solution.py:400

commit v5 on v4

--- a/solution.py
+++ b/solution.py
@@ -183,7 +183,7 @@
                 total = total + jnp.dot(
                     gamma[k, cut, pl.ds(4 * h, 4)].reshape(64, WIDE), virtp[4 * h + cut], preferred_element_type=F32
                 )
-        turned[:, k * 64 : (k + 1) * 64] = total.astype(BF16).astype(F32).T
+        turned[:, k * 64 : (k + 1) * 64] = total.T.astype(BF16)
 
     def lagrangian(k):
         for z in range(NZ):
@@ -264,8 +264,8 @@
     product(2, 1)
     opposite(3)
     product(2, 2)
+    sum_y(1)
     product(2, 3)
-    sum_y(1)
     from_sibling(3)
     product(3, 0)
     product(3, 1)
@@ -337,7 +337,7 @@
     copies = []
     for start in range(0, 375, 64):
         n = min(64, 375 - start)
-        spread = jnp.where(keep[None], turned[start : start + n][:, None, :], 0.0).astype(BF16)
+        spread = jnp.where(keep[None], turned[start : start + n].astype(F32)[:, None, :], 0.0).astype(BF16)
         value = jnp.dot(spread.reshape(n * ROWS, 256), weights[...], preferred_element_type=F32)
         out[start : start + n] = value.astype(BF16).reshape(n, ROWS, 128)
         rows = pl.ds(start, n)
@@ -356,7 +356,7 @@
         kernel,
         name="density",
         out_shape=(
-            jax.ShapeDtypeStruct((375, 256), F32),
+            jax.ShapeDtypeStruct((375, 256), BF16),
             jax.ShapeDtypeStruct((256, 128), BF16),
             jax.ShapeDtypeStruct((2, 16), F32),
         ),

time: 68.3 us -> 68.1 us (level)
  no operation moved by 1% of the time
where the time goes in v5:
time: 68.1 us; the launch traced here: 68 us
  Pallas kernels  67.4 us (99%)
    pallas_call x1, Pallas kernels, on_device(): pl.pallas_call(kernel, name='density', out_shape=(jax.ShapeDtypeStruct((3...  64 us
    pallas_call x1, Pallas kernels, on_device(): pl.pallas_call(second, name='second', out_shape=(jax.ShapeDtypeStruct((37...  3.39 us

profile of v5, /device:TPU:1, one launch (start us, length us, event | category | flops | bytes accessed | tf_op | source)
XLA Modules:
  0.0 68.0 jit_solution(14347805240299753870)
XLA Ops:
  0.6 64.0 %density.1 = (bf16[375,256]{1,0:T(8,128)(2,1)}, bf16[256,128]{1,0:T(8,128)(2,1)}, f32[2,16]{1,0:T(2,128)}) custom-call(bf16[900,3600]{1,0:T(8,128)(2,1)} %bitcast.5, bf16[16,3600]{1,0:T(8,128)(2,1)} %chol_hbm.1, bf16[1800,375]{1,0:T(8,128)(2,1)} %bitcast.6, bf16[16,128]{1,0:T(8,128)(2,1)} %bitcast.7), custom_call_target="tpu_custom_call" | custom-call | flops 5000000000 | bytes 12582912 | tf_op jit(solution)/shard_map/density/pallas_call | solution.py:355
  64.6 3.4 %second.1 = (bf16[375,16,128]{2,1,0:T(8,128)(2,1)}, f32[2,16]{1,0:T(2,128)}) custom-call(bf16[375,256]{1,0:T(8,128)(2,1)} %get-tuple-element.7.turned, bf16[256,128]{1,0:T(8,128)(2,1)} %get-tuple-element.8.weights, f32[2,16]{1,0:T(2,128)} %get-tuple-element.9.terms), custom_call_target="tpu_custom_call" | custom-call | flops 400000000 | bytes 2097152 | tf_op jit(solution)/shard_map/second/pallas_call | solution.py:400
